TPU v7x, 1024 devices: a whole 4x4x32 slice. The times are simulated.
1024 devices in a mesh: row: 32 (over z), col: 8 (over y, core), rep: 4 (over x).
Axes of the slice: x: 4, y: 4, z: 32, core: 2. Of those that a mesh axis runs over, the one named last changes fastest.
Arguments:
- density: bfloat16 [4096, 4096], P('row', 'col'), as said below
- block_mask: int32 [32, 32], replicated, may hold values from 0 to 1, as said below
- tile_order: int32 [32], replicated, may hold values from 0 to 31, as said below
Outputs:
- purified: bfloat16 [4096, 4096], P('row', 'col')
Inputs may be any that keep to these rules, and one draw needn't show every extreme that they name: `block_mask`: symmetric; ones on the diagonal and wherever the two block indices lie within 2 of each other around a circle of 32. `tile_order`: a permutation of the block indices. `density`: symmetric, and zero outside the blocks that block_mask keeps, read in stored order.
All inputs are finite; a program needn't handle non-finite values.
Results may differ from a plain program's by a relative error of at most 0.0041.
Values may be sent and summed in bfloat16 or wider, within the bound.
No kernel may reach another device: no remote copies, remote signals or barrier semaphores. Data moves between devices by JAX's collectives and lax.ppermute only.
A program may use at most 32 MiB of HBM per device.

v0:
```python
import jax
import jax.numpy as jnp
from jax import lax
from jax.sharding import PartitionSpec as P

TILE = 128
STEPS = 2


def body(density, block_mask, tile_order):
    height, breadth = density.shape
    layer_count = lax.axis_size("rep")
    layer_index = lax.axis_index("rep")
    row_count = lax.axis_size("row")
    row_index = lax.axis_index("row")
    col_index = lax.axis_index("col")
    blocks = block_mask.shape[0]
    onehot = (tile_order[:, None] == jnp.arange(blocks, dtype=jnp.int32)[None, :]).astype(
        jnp.float32
    )
    mask_float = block_mask.astype(jnp.float32)
    stored = jnp.dot(
        jnp.dot(onehot, mask_float, precision=lax.Precision.HIGHEST),
        onehot.T,
        precision=lax.Precision.HIGHEST,
    )
    block_rows = height // TILE
    block_cols = breadth // TILE
    local_blocks = lax.dynamic_slice(
        stored, (row_index * block_rows, col_index * block_cols), (block_rows, block_cols)
    )
    retain = jnp.broadcast_to(
        local_blocks[:, None, :, None], (block_rows, TILE, block_cols, TILE)
    ).reshape(height, breadth)

    def multiply(gathered_panel, operand):
        sub_rows = height // layer_count
        shaped = gathered_panel.reshape(height, row_count, layer_count, sub_rows)
        selected = lax.dynamic_index_in_dim(shaped, layer_index, 2, keepdims=False).reshape(
            height, row_count * sub_rows
        )
        portion_rows = lax.dynamic_slice_in_dim(operand, layer_index * sub_rows, sub_rows, 0)
        partial_sum = jnp.dot(
            selected,
            lax.all_gather(portion_rows, "row", axis=0, tiled=True),
            preferred_element_type=jnp.float32,
        )
        return lax.psum(partial_sum, "rep")

    matrix = density
    for step_number in range(STEPS):
        gathered_panel = lax.all_gather(matrix, "col", axis=1, tiled=True)
        square = multiply(gathered_panel, matrix)
        filtered = (retain * square).astype(jnp.bfloat16)
        cube = multiply(gathered_panel, filtered)
        matrix = (retain * (1.5 * matrix.astype(jnp.float32) - 0.5 * cube)).astype(jnp.bfloat16)
    return matrix


def solution(mesh):
    return jax.shard_map(
        body,
        mesh=mesh,
        in_specs=(P("row", "col"), P(), P()),
        out_specs=P("row", "col"),
        check_vma=False,
    )
```

profile of v0, /device:TPU:2, one launch (start us, length us, event | category | flops | bytes accessed | tf_op | source)
XLA Modules:
  0.0 956.5 jit_solution(13553386186660217974)
XLA Ops:
  6.5 1.7 copy.4
  8.3 0.8 copy-done.1
  9.8 0.6 copy-done.2
  10.9 48.1 %all-gather.7.cloned.1.call-done = bf16[128,4096]{0,1:T(8,128)(2,1)} async-done(((bf16[128,512]{0,1:T(8,128)(2,1)}), bf16[128,4096]{0,1:T(8,128)(2,1)}) %all-gather.7.cloned.1.call-update) | async-done | bytes 1048592 | tf_op jit(solution)/shard_map/all_gather | solution.py:52
  58.9 1.0 constant_dynamic-slice_fusion.3
  59.9 138.4 %all-gather.9.cloned.1.call-done = bf16[1024,512]{1,0:T(8,128)(2,1)} async-done(((bf16[32,512]{1,0:T(8,128)(2,1)}), bf16[1024,512]{1,0:T(8,128)(2,1)}) %all-gather.9.cloned.1.call-update) | async-done | bytes 1048592 | tf_op jit(solution)/shard_map/all_gather | solution.py:45
  198.3 2.3 fusion.7
  200.8 69.1 %all-reduce.5.cloned.1.call-done = f32[128,512]{1,0:T(8,128)} async-done(((f32[128,512]{1,0:T(8,128)}), f32[128,512]{1,0:T(8,128)}) %all-reduce.5.cloned.1.call-update) | async-done | bytes 262160 | tf_op jit(solution)/shard_map/psum | solution.py:48
  270.0 1.5 fusion.1
  271.5 138.2 %all-gather.11.cloned.1.call-done = bf16[1024,512]{1,0:T(8,128)(2,1)} async-done(((bf16[32,512]{1,0:T(8,128)(2,1)}), bf16[1024,512]{1,0:T(8,128)(2,1)}) %all-gather.11.cloned.1.call-update) | async-done | bytes 1048592 | tf_op jit(solution)/shard_map/all_gather | solution.py:45
  409.7 2.3 fusion.8
  412.0 69.3 %all-reduce.7.cloned.1.call-done = f32[128,512]{1,0:T(8,128)} async-done(((f32[128,512]{1,0:T(8,128)}), f32[128,512]{1,0:T(8,128)}) %all-reduce.7.cloned.1.call-update) | async-done | bytes 262160 | tf_op jit(solution)/shard_map/psum | solution.py:48
  481.4 1.7 multiply_convert_fusion.1
  483.1 0.8 copy-done
  484.6 40.8 %all-gather.13.cloned.1.call-done = bf16[128,4096]{1,0:T(8,128)(2,1)} async-done(((bf16[128,512]{1,0:T(8,128)(2,1)}), bf16[128,4096]{1,0:T(8,128)(2,1)}) %all-gather.13.cloned.1.call-update) | async-done | bytes 1048592 | tf_op jit(solution)/shard_map/all_gather | solution.py:52
  525.4 1.6 copy.5
  527.1 137.8 %all-gather.15.cloned.1.call-done = bf16[1024,512]{1,0:T(8,128)(2,1)} async-done(((bf16[32,512]{1,0:T(8,128)(2,1)}), bf16[1024,512]{1,0:T(8,128)(2,1)}) %all-gather.15.cloned.1.call-update) | async-done | bytes 1048592 | tf_op jit(solution)/shard_map/all_gather | solution.py:45
  664.8 2.3 fusion.9
  667.2 69.3 %all-reduce.9.cloned.1.call-done = f32[128,512]{1,0:T(8,128)} async-done(((f32[128,512]{1,0:T(8,128)}), f32[128,512]{1,0:T(8,128)}) %all-reduce.9.cloned.1.call-update) | async-done | bytes 262160 | tf_op jit(solution)/shard_map/psum | solution.py:48
  736.5 1.5 fusion
  738.0 138.4 %all-gather.17.cloned.1.call-done = bf16[1024,512]{1,0:T(8,128)(2,1)} async-done(((bf16[32,512]{1,0:T(8,128)(2,1)}), bf16[1024,512]{1,0:T(8,128)(2,1)}) %all-gather.17.cloned.1.call-update) | async-done | bytes 1048592 | tf_op jit(solution)/shard_map/all_gather | solution.py:45
  876.4 2.3 fusion.10
  878.6 69.4 %all-reduce.11.cloned.1.call-done = f32[128,512]{1,0:T(8,128)} async-done(((f32[128,512]{1,0:T(8,128)}), f32[128,512]{1,0:T(8,128)}) %all-reduce.11.cloned.1.call-update) | async-done | bytes 262160 | tf_op jit(solution)/shard_map/psum | solution.py:48
  948.0 1.7 multiply_convert_fusion
  (32 shorter events, 2.4 us)
Async XLA Ops:
  6.5 52.4 %all-gather.7.cloned.1.call-start = ((), (), s32[]{:S(2)}) async-start(), calls=%async_computation | async-start | bytes 1179648 | tf_op jit(solution)/shard_map/all_gather | solution.py:52
  8.2 0.9 copy-start.1
  8.2 190.1 %all-gather.9.cloned.1.call-start = ((), (), s32[]{:S(2)}) async-start(), calls=%async_computation.1 | async-start | bytes 1081344 | tf_op jit(solution)/shard_map/all_gather | solution.py:45
  9.7 0.7 copy-start.2
  9.8 260.2 %all-reduce.5.cloned.1.call-start = ((), (), s32[]{:S(2)}) async-start(), calls=%async_computation.2 | async-start | bytes 524288 | tf_op jit(solution)/shard_map/psum | solution.py:48
  9.8 0.7 copy-start.3
  200.6 209.1 %all-gather.11.cloned.1.call-start = ((), (), s32[]{:S(2)}) async-start(), calls=%async_computation.3 | async-start | bytes 1081344 | tf_op jit(solution)/shard_map/all_gather | solution.py:45
  271.4 209.9 %all-reduce.7.cloned.1.call-start = ((), (), s32[]{:S(2)}) async-start(), calls=%async_computation.4 | async-start | bytes 524288 | tf_op jit(solution)/shard_map/psum | solution.py:48
  412.0 113.4 %all-gather.13.cloned.1.call-start = ((), (), s32[]{:S(2)}) async-start(), calls=%async_computation.5 | async-start | bytes 1179648 | tf_op jit(solution)/shard_map/all_gather | solution.py:52
  483.0 0.9 copy-start
  483.1 181.8 %all-gather.15.cloned.1.call-start = ((), (), s32[]{:S(2)}) async-start(), calls=%async_computation.6 | async-start | bytes 1081344 | tf_op jit(solution)/shard_map/all_gather | solution.py:45
  484.6 251.9 %all-reduce.9.cloned.1.call-start = ((), (), s32[]{:S(2)}) async-start(), calls=%async_computation.7 | async-start | bytes 524288 | tf_op jit(solution)/shard_map/psum | solution.py:48
  667.1 209.2 %all-gather.17.cloned.1.call-start = ((), (), s32[]{:S(2)}) async-start(), calls=%async_computation.8 | async-start | bytes 1081344 | tf_op jit(solution)/shard_map/all_gather | solution.py:45
  737.9 210.1 %all-reduce.11.cloned.1.call-start = ((), (), s32[]{:S(2)}) async-start(), calls=%async_computation.9 | async-start | bytes 524288 | tf_op jit(solution)/shard_map/psum | solution.py:48
Sparse Core Ops, SparseCore 0:
  10.1 48.7 all-gather.6
  61.6 136.7 all-gather.8
  200.7 69.1 all-reduce.4
  272.8 136.8 all-gather.10
  412.1 69.2 all-reduce.6
  483.9 41.4 all-gather.12
  528.1 136.7 all-gather.14
  667.2 69.1 all-reduce.8
  739.5 136.8 all-gather.16
  878.8 69.1 all-reduce.10
where the time goes:
time: 957 us
  waiting for transfers between devices  919 us (96%)
  between operations  13.6 us (1%)
    all_gather x4, waiting for transfers between devices, multiply(): lax.all_gather(portion_rows, 'row', axis=0, tiled=True)  553 us
    psum x4, waiting for transfers between devices, multiply(): return lax.psum(partial_sum, 'rep')  277 us
    all_gather x2, waiting for transfers between devices, body(): gathered_panel = lax.all_gather(matrix, 'col', axis=1, tiled=True)  88.9 us
  transfers between devices with their start and end apart: 10, of which 10 were waited for; matrix products, arithmetic and copies ran while one was open for 0% of the time, Pallas kernels for 0%

commit v1 on v0

--- a/solution.py
+++ b/solution.py
@@ -1,29 +1,29 @@
 import jax
 import jax.numpy as jnp
 from jax import lax
+from jax.experimental import pallas as pl
+from jax.experimental.pallas import tpu as pltpu
 from jax.sharding import PartitionSpec as P
 
 TILE = 128
 STEPS = 2
-
-
-def body(density, block_mask, tile_order):
+CHUNK = 16
+CLASSES = 4
+PER_ROW = 3
+CLASS_CAP = 44
+HALF = CLASSES * CLASS_CAP
+NEAR = 16
+GROUP = 8
+ZERO = 2 * HALF
+
+
+def dense(density, stored):
     height, breadth = density.shape
     layer_count = lax.axis_size("rep")
     layer_index = lax.axis_index("rep")
     row_count = lax.axis_size("row")
     row_index = lax.axis_index("row")
     col_index = lax.axis_index("col")
-    blocks = block_mask.shape[0]
-    onehot = (tile_order[:, None] == jnp.arange(blocks, dtype=jnp.int32)[None, :]).astype(
-        jnp.float32
-    )
-    mask_float = block_mask.astype(jnp.float32)
-    stored = jnp.dot(
-        jnp.dot(onehot, mask_float, precision=lax.Precision.HIGHEST),
-        onehot.T,
-        precision=lax.Precision.HIGHEST,
-    )
     block_rows = height // TILE
     block_cols = breadth // TILE
     local_blocks = lax.dynamic_slice(
@@ -57,6 +57,289 @@
     return matrix
 
 
+def exact_dot(a, b):
+    return jnp.dot(
+        a.astype(jnp.bfloat16), b.astype(jnp.bfloat16), preferred_element_type=jnp.float32
+    )
+
+
+def tables(stored, tile_order, row, col, rep):
+    nb = stored.shape[0]
+    kept = stored > 0.5
+    index = jnp.arange(nb, dtype=jnp.int32)
+    before = (index[:, None] < index[None, :]).astype(jnp.float32)
+    apart = (tile_order[None, :] - tile_order[:, None]) % nb
+    mine = (apart < nb // 2) | ((apart == nb // 2) & (tile_order[:, None] < nb // 2))
+    own = (kept & mine).astype(jnp.float32)
+    rank = exact_dot(own, before).astype(jnp.int32)
+    owned = jnp.sum(own, axis=1).astype(jnp.int32)
+    classes = jnp.arange(CLASSES, dtype=jnp.int32)
+    first = (classes[:, None] - index[None, :]) % CLASSES
+    count = (owned[None, :] - first + CLASSES - 1) // CLASSES
+    base = jnp.sum(
+        jnp.where(index[None, None, :] < index[None, :, None], count[:, None, :], 0), axis=2
+    )
+    total = jnp.sum(count, axis=1)
+    wanted = jnp.arange(PER_ROW, dtype=jnp.int32) * CLASSES + (rep - row) % CLASSES
+    row_own = lax.dynamic_index_in_dim(own, row, 0, keepdims=False) > 0.5
+    row_rank = lax.dynamic_index_in_dim(rank, row, 0, keepdims=False)
+    hit = row_own[None, :] & (row_rank[None, :] == wanted[:, None])
+    send = jnp.sum(jnp.where(hit, index[None, :] + 1, 0), axis=1) - 1
+    my_base = lax.dynamic_index_in_dim(base, rep, 0, keepdims=False)
+    my_count = lax.dynamic_index_in_dim(count, rep, 0, keepdims=False)
+    place = jnp.arange(CLASS_CAP, dtype=jnp.int32)[:, None]
+    inside = (place >= my_base[None, :]) & (place < (my_base + my_count)[None, :])
+    keep = (
+        jnp.sum(
+            jnp.where(inside, index[None, :] * PER_ROW + place - my_base[None, :] + 1, 0), axis=1
+        )
+        - 1
+    )
+    which = (rank + index[:, None]) % CLASSES
+    start = jnp.zeros_like(rank)
+    for c in range(CLASSES):
+        start = jnp.where(which == c, base[c][:, None] + c * CLASS_CAP, start)
+    slot = start + rank // CLASSES
+    slots = jnp.where(own > 0.5, slot, jnp.where(kept, slot.T + HALF, ZERO))
+    a = stored
+    er = lax.dynamic_index_in_dim(stored, row, 0, keepdims=False)
+    k_set = er * ((index // (nb // 8)) == col)
+    through = exact_dot(a * k_set[None, :], a)
+    need_x = kept & ((k_set[None, :] > 0.5) | ((er[:, None] > 0.5) & (through > 0.5)))
+    need_f = kept & (exact_dot(a, need_x) > 0.5)
+    x_slots = jnp.where(need_x, slots, ZERO)
+    f_slots = jnp.where(need_f, slots, ZERO)
+    pad = lambda t: jnp.pad(t, ((0, 1), (0, 1)), constant_values=ZERO)
+    near_rank = exact_dot(a, before).astype(jnp.int32)
+    steps = jnp.arange(NEAR, dtype=jnp.int32)
+    near_hit = kept[:, None, :] & (near_rank[:, None, :] == steps[None, :, None])
+    near = jnp.sum(jnp.where(near_hit, index[None, None, :] - nb, 0), axis=2) + nb
+    near_count = jnp.sum(kept.astype(jnp.int32), axis=1)
+    fits = (
+        (jnp.max(owned) <= PER_ROW * CLASSES)
+        & (jnp.max(total) <= CLASS_CAP)
+        & (jnp.max(near_count) <= NEAR)
+    )
+    return fits, dict(
+        send=send,
+        keep=keep,
+        slots=pad(slots),
+        x_slots=pad(x_slots),
+        f_slots=pad(f_slots),
+        near=near,
+        near_count=near_count,
+        total=total,
+    )
+
+
+def pick_kernel(send_ref, got_ref, out_ref):
+    for t in range(PER_ROW):
+        b = send_ref[t]
+        at = jnp.maximum(b, 0)
+        tile = got_ref[at // 4, :, pl.ds(pl.multiple_of((at % 4) * TILE, TILE), TILE)]
+        out_ref[t] = jnp.where(b >= 0, tile, jnp.zeros_like(tile))
+
+
+def pack_kernel(keep_ref, all_ref, out_ref):
+    def one(p, carry):
+        e = keep_ref[p]
+        tile = all_ref[jnp.maximum(e, 0)]
+        out_ref[p] = jnp.where(e >= 0, tile, jnp.zeros_like(tile))
+        return carry
+
+    lax.fori_loop(0, CLASS_CAP, one, 0, unroll=4)
+
+
+def purify_kernel(
+    place_ref,
+    total_ref,
+    slots_ref,
+    x_slots_ref,
+    f_slots_ref,
+    near_ref,
+    near_count_ref,
+    own_ref,
+    other_ref,
+    out_ref,
+    w,
+    f,
+    x,
+    sems,
+):
+    row, col, core = place_ref[0], place_ref[1], place_ref[2]
+    nb = 32
+
+    def copies():
+        for part, (ref, half) in enumerate(((own_ref, core), (other_ref, 1 - core))):
+            for q in range(CLASSES):
+                for y in range(4):
+                    yield pltpu.make_async_copy(
+                        ref.at[q * 4 + y],
+                        w.at[pl.ds(q * CLASS_CAP, CLASS_CAP), 2 * y + half],
+                        sems.at[part * 16 + q * 4 + y],
+                    )
+
+    for c in copies():
+        c.start()
+    zero = jnp.zeros((TILE, TILE), jnp.bfloat16)
+    w[ZERO] = zero.reshape(8, CHUNK, TILE)
+    f[ZERO] = zero
+    x[ZERO] = zero
+    for c in copies():
+        c.wait()
+
+    def w_at(s):
+        return w[s].reshape(TILE, TILE)
+
+    for q in range(CLASSES):
+
+        def turn(p, carry, q=q):
+            s = q * CLASS_CAP + p
+            w[s + HALF] = w_at(s).T.reshape(8, CHUNK, TILE)
+            return carry
+
+        lax.fori_loop(0, total_ref[q], turn, 0)
+
+    def product(i, j, left, left_slots, right, right_slots):
+        def some(g):
+            ls = [near_ref[j, g * GROUP + t] for t in range(GROUP)]
+            lhs = jnp.concatenate([left(left_slots[i, l]) for l in ls], axis=1)
+            rhs = jnp.concatenate([right(right_slots[l, j]) for l in ls], axis=0)
+            return jnp.dot(lhs, rhs, preferred_element_type=jnp.float32)
+
+        return lax.cond(
+            near_count_ref[j] > GROUP, lambda: some(0) + some(1), lambda: some(0)
+        )
+
+    f_at = lambda s: f[s]
+    x_at = lambda s: x[s]
+
+    def f_column(j, carry):
+        def one(t, carry):
+            i = near_ref[j, t]
+            s = f_slots_ref[i, j]
+
+            @pl.when(s != ZERO)
+            def _():
+                f[s] = product(i, j, w_at, slots_ref, w_at, slots_ref).astype(jnp.bfloat16)
+
+            return carry
+
+        return lax.fori_loop(0, near_count_ref[j], one, carry)
+
+    lax.fori_loop(0, nb, f_column, 0)
+
+    def x_column(j, carry):
+        def one(t, carry):
+            i = near_ref[j, t]
+            s = x_slots_ref[i, j]
+
+            @pl.when(s != ZERO)
+            def _():
+                cube = product(i, j, w_at, slots_ref, f_at, f_slots_ref)
+                x[s] = (1.5 * w_at(s).astype(jnp.float32) - 0.5 * cube).astype(jnp.bfloat16)
+
+            return carry
+
+        return lax.fori_loop(0, near_count_ref[j], one, carry)
+
+    lax.fori_loop(0, nb, x_column, 0)
+
+    for b in range(4):
+        k = col * 4 + b
+        own = slots_ref[row, k]
+
+        def one(t, total, k=k):
+            m = near_ref[k, t]
+
+            def add():
+                square = product(m, k, x_at, x_slots_ref, x_at, x_slots_ref).astype(jnp.bfloat16)
+                return total + jnp.dot(
+                    x[x_slots_ref[row, m]], square, preferred_element_type=jnp.float32
+                )
+
+            return lax.cond(slots_ref[row, m] != ZERO, add, lambda: total)
+
+        trips = jnp.where(own != ZERO, near_count_ref[k], 0)
+        cube = lax.fori_loop(0, trips, one, jnp.zeros((TILE, TILE), jnp.float32))
+        mine = jnp.where(own != ZERO, x_slots_ref[row, k], ZERO)
+        out_ref[:, b * TILE : (b + 1) * TILE] = (
+            1.5 * x[mine].astype(jnp.float32) - 0.5 * cube
+        ).astype(jnp.bfloat16)
+
+
+SMEM = pl.BlockSpec(memory_space=pltpu.SMEM)
+VMEM = pl.BlockSpec(memory_space=pltpu.VMEM)
+ANY = pl.BlockSpec(memory_space=pl.ANY)
+
+
+def sparse(density, table, row, col, rep):
+    bf16 = jnp.bfloat16
+    rows = lax.axis_size("row")
+    got = lax.all_to_all(density.reshape(8, CHUNK, 4 * TILE), "col", 0, 0)
+    picked = pl.pallas_call(
+        pick_kernel,
+        out_shape=jax.ShapeDtypeStruct((PER_ROW, CHUNK, TILE), bf16),
+        in_specs=[SMEM, VMEM],
+        out_specs=VMEM,
+    )(table["send"], got)
+    everywhere = lax.all_gather(picked, "row", axis=0, tiled=True)
+    packed = pl.pallas_call(
+        pack_kernel,
+        out_shape=jax.ShapeDtypeStruct((CLASS_CAP, CHUNK, TILE), bf16),
+        in_specs=[SMEM, VMEM],
+        out_specs=VMEM,
+    )(table["keep"], everywhere)
+    groups = [[q * 8 + c for q in range(4) for c in range(k, 8, 2)] for k in (0, 1)]
+    own = lax.all_to_all(
+        jnp.broadcast_to(packed[None], (16,) + packed.shape),
+        ("rep", "col"),
+        0,
+        0,
+        axis_index_groups=groups,
+    )
+    other = lax.ppermute(own, "col", [(i, i ^ 1) for i in range(8)])
+    place = jnp.stack([row, col, col % 2]).astype(jnp.int32)
+    return pl.pallas_call(
+        purify_kernel,
+        out_shape=jax.ShapeDtypeStruct((TILE, 4 * TILE), bf16),
+        in_specs=[SMEM] * 7 + [ANY, ANY],
+        out_specs=VMEM,
+        scratch_shapes=[
+            pltpu.VMEM((ZERO + 1, 8, CHUNK, TILE), bf16),
+            pltpu.VMEM((ZERO + 1, TILE, TILE), bf16),
+            pltpu.VMEM((ZERO + 1, TILE, TILE), bf16),
+            pltpu.SemaphoreType.DMA((32,)),
+        ],
+        compiler_params=pltpu.CompilerParams(vmem_limit_bytes=44 * 1024 * 1024),
+    )(
+        place,
+        table["total"],
+        table["slots"],
+        table["x_slots"],
+        table["f_slots"],
+        table["near"],
+        table["near_count"],
+        own,
+        other,
+    )
+
+
+def body(density, block_mask, tile_order):
+    row, col, rep = (lax.axis_index(a) for a in ("row", "col", "rep"))
+    blocks = block_mask.shape[0]
+    onehot = (tile_order[:, None] == jnp.arange(blocks, dtype=jnp.int32)[None, :]).astype(
+        jnp.float32
+    )
+    stored = exact_dot(exact_dot(onehot, block_mask), onehot.T)
+    fits, table = tables(stored, tile_order, row, col, rep)
+    return lax.cond(
+        fits,
+        lambda: sparse(density, table, row, col, rep),
+        lambda: dense(density, stored),
+    )
+
+
 def solution(mesh):
     return jax.shard_map(
         body,

time: 957 us -> 209 us (0.22)
  waiting for transfers between devices: 919 us -> 8.96 us
  blocking collectives: 0 us -> 101 us
  Pallas kernels: 0 us -> 61.5 us
    all_gather x6 -> x0, waiting for transfers between devices: 642 us -> none  [the longest x4 553 us: multiply(): lax.all_gather(portion_rows, 'row', axis=0, tiled=True)]
    psum x4 -> x0, waiting for transfers between devices: 277 us -> none  [multiply(): return lax.psum(partial_sum, 'rep')]
    all_gather x0 -> x1, blocking collectives: none -> 75.2 us  [sparse(): everywhere = lax.all_gather(picked, 'row', axis=0, tiled=True)]
    pallas_call x0 -> x3, Pallas kernels: none -> 61.5 us  [the longest x1 58.2 us: sparse(): pl.pallas_call(purify_kernel, out_shape=jax.ShapeDtypeStruct((TILE, 4 * T...]
    all_to_all x0 -> x1, blocking collectives: none -> 26.1 us  [sparse(): lax.all_to_all(jnp.broadcast_to(packed[None], (16,) + packed.shape), ('re...]
  transfers between devices with their start and end apart: 10 -> 2, of which waited for: 10 -> 2; matrix products, arithmetic and copies ran while one was open for 0% -> 1% of each run, Pallas kernels for 0% -> 0%
where the time goes in v1:
time: 209 us
  blocking collectives  101 us (48%)
  Pallas kernels  61.5 us (29%)
  between operations  15.5 us (7%)
  waiting for transfers between devices  8.96 us (4%)
  other arithmetic  6.76 us (3%)
  starting transfers between devices  6.38 us (3%)
  local copies, waits for them, and re-layouts  5.72 us (3%)
  matrix products  2.26 us (1%)
    all_gather x1, blocking collectives, sparse(): everywhere = lax.all_gather(picked, 'row', axis=0, tiled=True)  75.2 us
    pallas_call x1, Pallas kernels, sparse(): pl.pallas_call(purify_kernel, out_shape=jax.ShapeDtypeStruct((TILE, 4 * T...  58.2 us
    all_to_all x1, blocking collectives, sparse(): lax.all_to_all(jnp.broadcast_to(packed[None], (16,) + packed.shape), ('re...  26.1 us
    all_to_all x1, waiting for transfers between devices, sparse(): got = lax.all_to_all(density.reshape(8, CHUNK, 4 * TILE), 'col', 0, 0)  4.62 us
    all_to_all x1, starting transfers between devices, sparse(): got = lax.all_to_all(density.reshape(8, CHUNK, 4 * TILE), 'col', 0, 0)  4.47 us
    ppermute x1, waiting for transfers between devices, sparse(): other = lax.ppermute(own, 'col', [(i, i ^ 1) for i in range(8)])  4.33 us
  transfers between devices with their start and end apart: 2, of which 2 were waited for; matrix products, arithmetic and copies ran while one was open for 1% of the time, Pallas kernels for 0%

profile of v1, /device:TPU:2, one launch (start us, length us, event | category | flops | bytes accessed | tf_op | source)
XLA Modules:
  0.0 208.7 jit_solution(15569197609062658437)
XLA Ops:
  6.5 0.7 broadcast_compare_fusion.3
  7.2 1.1 convert_reduce_fusion
  8.4 0.6 reduce_max.29
  9.9 0.7 convolution_convert_fusion
  10.7 0.9 fusion.52
  11.6 0.6 convert_reduce_fusion.1
  13.0 0.6 reduce_max.28
  14.5 0.6 slice_bitcast_fusion
  16.3 0.6 eq.123
  17.5 0.6 broadcast.298
  18.1 183.0 %conditional.1 = (bf16[128,512]{1,0:T(8,128)(2,1)S(1)}) conditional(s32[]{:T(128)} %convert_element_type.95, (f32[32,32]{1,0:T(8,128)S(1)}, bf16[128,512]{1,0:T(8,128)(2,1)}) %tuple.11, (s32[]{:T(128)}, s32[]{:T(128)}, bf16[128,512]{1,0:T(8,128)(2,1)}, f32[32,32]{1,0:T(8,128)S(1)}, s32[44,32]{1,0:T(8,128)S(1)}, /*index=5*/s32[4]{0:T(128)}, ...), branch_computations={%region_10.15_spmd, %region_15.16_spmd} | conditional | flops 537985024 | bytes 38480660 | solution.py:336
  18.2 4.5 %all-to-all-start = ((bf16[8,16,512]{2,1,0:T(8,128)(2,1)}), bf16[8,16,512]{2,1,0:T(8,128)(2,1)S(1)}, u32[]{:S(2)}, u32[]{:S(2)}) async-start(bf16[8,16,512]{2,1,0:T(8,128)(2,1)} %bitcast.53), calls=%async_computation | async-start | bytes 262144 | tf_op jit(solution)/shard_map/cond/branch_1_fun/all_to_all | solution.py:279
  24.1 4.6 %all-to-all-done.got_ref = bf16[8,16,512]{2,1,0:T(8,128)(2,1)S(1)} async-done(((bf16[8,16,512]{2,1,0:T(8,128)(2,1)}), bf16[8,16,512]{2,1,0:T(8,128)(2,1)S(1)}, u32[]{:S(2)}, u32[]{:S(2)}) %all-to-all-start) | async-done | bytes 131104 | tf_op jit(solution)/shard_map/cond/branch_1_fun/all_to_all | solution.py:279
  28.8 0.7 copy-done.2
  29.4 1.5 branch_1_fun.3
  30.9 75.2 %all_gather.20.all_ref = bf16[96,16,128]{2,1,0:T(8,128)(2,1)} all-gather(bf16[3,16,128]{2,1,0:T(8,128)(2,1)} %branch_1_fun.3), channel_id=1, replica_groups=mesh['row'=32,'col'=8,'rep'=4] {'row'}, dimensions={0}, use_global_device_ids=true | all-gather | bytes 405504 | tf_op jit(solution)/shard_map/cond/branch_1_fun/all_gather | solution.py:286
  106.2 1.8 branch_1_fun.4
  108.0 1.5 broadcast_in_dim.116
  109.6 26.1 %all_to_all.8.own_ref = bf16[16,44,16,128]{3,2,1,0:T(8,128)(2,1)S(1)} all-to-all(bf16[16,44,16,128]{3,2,1,0:T(8,128)(2,1)S(1)} %broadcast_in_dim.116), channel_id=1, replica_groups={{0,8,16,24,1,9,17,25,2,10,18,26,3,11,19,27},{4,12,20,28,5,13,21,29,6,14..., dimensions={0} | all-to-all | bytes 5767168 | tf_op jit(solution)/shard_map/cond/branch_1_fun/all_to_all | solution.py:294
  135.7 1.9 collective-permute-start
  138.0 0.6 select_reduce_fusion
  138.6 4.3 %collective-permute-done.other_ref = bf16[16,44,16,128]{3,2,1,0:T(8,128)(2,1)} collective-permute-done((bf16[16,44,16,128]{3,2,1,0:T(8,128)(2,1)S(1)}, bf16[16,44,16,128]{3,2,1,0:T(8,128)(2,1)}, u32[]{:S(2)}, u32[]{:S(2)}) %collective-permute-start) | collective-permute-done | bytes 2883616 | tf_op jit(solution)/shard_map/cond/branch_1_fun/ppermute | solution.py:301
  143.0 58.2 %branch_1_fun.5 = bf16[128,512]{1,0:T(8,128)(2,1)S(1)} custom-call(s32[3]{0:T(128)S(1)} %pad_add_fusion.place_ref, s32[4]{0:T(128)} %get-tuple-element.38.total_ref, s32[33,33]{1,0:T(8,128)S(1)} %pad.13.slots_ref, s32[33,33]{1,0:T(8,128)S(1)} %pad.14.x_slots_ref, s32[33,33]{1,0:T(8,128)S(1)} %pad.15.f_slots_ref, s32[32,16]{1,0:T(8,128)S(1)} %broadcast_add_fusion.near_ref, ...), custom_call_target="tpu_custom_call" | custom-call | tf_op jit(solution)/shard_map/cond/branch_1_fun/pallas_call | solution.py:303
  201.2 0.6 copy-done.3
  (70 shorter events, 4.2 us)
Async XLA Ops:
  8.4 1.6 copy-start.14
  13.0 1.3 copy-start.13
  18.2 10.6 %all-to-all-start = ((bf16[8,16,512]{2,1,0:T(8,128)(2,1)}), bf16[8,16,512]{2,1,0:T(8,128)(2,1)S(1)}, u32[]{:S(2)}, u32[]{:S(2)}) async-start(bf16[8,16,512]{2,1,0:T(8,128)(2,1)} %bitcast.53), calls=%async_computation | async-start | bytes 262144 | tf_op jit(solution)/shard_map/cond/branch_1_fun/all_to_all | solution.py:279
  28.8 0.7 copy-start.2
  109.5 28.2 %copy-start.5 = (s32[32,32]{1,0:T(8,128)S(1)}, s32[32,32]{1,0:T(8,128)}, u32[]{:S(2)}) copy-start(s32[32,32]{1,0:T(8,128)} %get-tuple-element.343) | copy-start | bytes 12292 | tf_op jit(solution)/shard_map/cond
  109.5 28.2 %copy-start.6 = (s32[32,32]{1,0:T(8,128)S(1)}, s32[32,32]{1,0:T(8,128)}, u32[]{:S(2)}) copy-start(s32[32,32]{1,0:T(8,128)} %get-tuple-element.344) | copy-start | bytes 12292 | tf_op jit(solution)/shard_map/cond
  109.5 28.2 %copy-start.7 = (s32[32,32]{1,0:T(8,128)S(1)}, s32[32,32]{1,0:T(8,128)}, u32[]{:S(2)}) copy-start(s32[32,32]{1,0:T(8,128)} %get-tuple-element.345) | copy-start | bytes 12292 | tf_op jit(solution)/shard_map/cond
  109.5 28.2 %copy-start.8 = (s32[32,32]{1,0:T(8,128)S(1)}, s32[32,32]{1,0:T(8,128)}, u32[]{:S(2)}) copy-start(s32[32,32]{1,0:T(8,128)} %get-tuple-element.346) | copy-start | bytes 12292 | tf_op jit(solution)/shard_map/cond
  109.5 28.2 %copy-start.9 = (s32[32]{0:T(128)S(1)}, s32[32]{0:T(128)}, u32[]{:S(2)}) copy-start(s32[32]{0:T(128)} %get-tuple-element.261) | copy-start | bytes 388 | tf_op jit(solution)/shard_map/cond
  109.5 28.2 %copy-start.10 = (s32[32]{0:T(128)S(1)}, s32[32]{0:T(128)}, u32[]{:S(2)}) copy-start(s32[32]{0:T(128)} %get-tuple-element.251) | copy-start | bytes 388 | tf_op jit(solution)/shard_map/cond
  109.5 28.2 %copy-start.11 = (s32[32]{0:T(128)S(1)}, s32[32]{0:T(128)}, u32[]{:S(2)}) copy-start(s32[32]{0:T(128)} %get-tuple-element.241) | copy-start | bytes 388 | tf_op jit(solution)/shard_map/cond
  109.6 28.2 %copy-start.12 = (s32[32]{0:T(128)S(1)}, s32[32]{0:T(128)}, u32[]{:S(2)}) copy-start(s32[32]{0:T(128)} %get-tuple-element.227) | copy-start | bytes 388 | tf_op jit(solution)/shard_map/cond
  109.6 28.4 %copy-start.4 = (s32[32,32]{1,0:T(8,128)S(1)}, s32[32,32]{1,0:T(8,128)}, u32[]{:S(2)}) copy-start(s32[32,32]{1,0:T(8,128)} %get-tuple-element.125) | copy-start | bytes 12292 | tf_op jit(solution)/shard_map/cond
  135.7 7.3 %collective-permute-start = (bf16[16,44,16,128]{3,2,1,0:T(8,128)(2,1)S(1)}, bf16[16,44,16,128]{3,2,1,0:T(8,128)(2,1)}, u32[]{:S(2)}, u32[]{:S(2)}) collective-permute-start(bf16[16,44,16,128]{3,2,1,0:T(8,128)(2,1)S(1)} %all_to_all.8.own_ref), channel_id=1, source_target_pairs={{0,4},{4,0},{8,12},{12,8},{16,20},{20,16},{24,28},{28,24},{1,5},{5... | collective-permute-start | bytes 8650760 | tf_op jit(solution)/shard_map/cond/branch_1_fun/ppermute | solution.py:301
  201.2 0.7 copy-start.3

commit v2 on v1

v2 whole, which is shorter than its diff:
```python
import jax
import jax.numpy as jnp
from jax import lax
from jax.experimental import pallas as pl
from jax.experimental.pallas import tpu as pltpu
from jax.sharding import PartitionSpec as P

TILE = 128
STEPS = 2
CHUNK = 16
CLASSES = 4
PER_ROW = 3
CLASS_CAP = 40
HALF = CLASSES * CLASS_CAP
GROUP = 4
PAIRS = 6
TURN = 10
ZERO = 2 * HALF


def dense(density, stored):
    height, breadth = density.shape
    layer_count = lax.axis_size("rep")
    layer_index = lax.axis_index("rep")
    row_count = lax.axis_size("row")
    row_index = lax.axis_index("row")
    col_index = lax.axis_index("col")
    block_rows = height // TILE
    block_cols = breadth // TILE
    local_blocks = lax.dynamic_slice(
        stored, (row_index * block_rows, col_index * block_cols), (block_rows, block_cols)
    )
    retain = jnp.broadcast_to(
        local_blocks[:, None, :, None], (block_rows, TILE, block_cols, TILE)
    ).reshape(height, breadth)

    def multiply(gathered_panel, operand):
        sub_rows = height // layer_count
        shaped = gathered_panel.reshape(height, row_count, layer_count, sub_rows)
        selected = lax.dynamic_index_in_dim(shaped, layer_index, 2, keepdims=False).reshape(
            height, row_count * sub_rows
        )
        portion_rows = lax.dynamic_slice_in_dim(operand, layer_index * sub_rows, sub_rows, 0)
        partial_sum = jnp.dot(
            selected,
            lax.all_gather(portion_rows, "row", axis=0, tiled=True),
            preferred_element_type=jnp.float32,
        )
        return lax.psum(partial_sum, "rep")

    matrix = density
    for step_number in range(STEPS):
        gathered_panel = lax.all_gather(matrix, "col", axis=1, tiled=True)
        square = multiply(gathered_panel, matrix)
        filtered = (retain * square).astype(jnp.bfloat16)
        cube = multiply(gathered_panel, filtered)
        matrix = (retain * (1.5 * matrix.astype(jnp.float32) - 0.5 * cube)).astype(jnp.bfloat16)
    return matrix


def exact_dot(a, b):
    return jnp.dot(
        a.astype(jnp.bfloat16), b.astype(jnp.bfloat16), preferred_element_type=jnp.float32
    )


def owners(stored, tile_order):
    nb = stored.shape[0]
    index = jnp.arange(nb, dtype=jnp.int32)
    apart = (tile_order[None, :] - tile_order[:, None]) % nb
    mine = (apart < nb // 2) | ((apart == nb // 2) & (tile_order[:, None] < nb // 2))
    own = jnp.where(mine, stored, 0)
    owned = jnp.sum(own, axis=1).astype(jnp.int32)
    classes = jnp.arange(CLASSES, dtype=jnp.int32)
    first = (classes[:, None] - index[None, :]) % CLASSES
    count = (owned[None, :] - first + CLASSES - 1) // CLASSES
    total = jnp.sum(count, axis=1)
    over = jnp.concatenate([owned - PER_ROW * CLASSES, total - CLASS_CAP])
    return own, count, jnp.max(over) <= 0


def tables(stored, own, count, row, col, rep):
    nb = stored.shape[0]
    kept = stored > 0.5
    index = jnp.arange(nb, dtype=jnp.int32)
    before = (index[:, None] < index[None, :]).astype(jnp.float32)
    rank = exact_dot(own, before).astype(jnp.int32)
    total = jnp.sum(count, axis=1)
    base = jnp.sum(
        jnp.where(index[None, None, :] < index[None, :, None], count[:, None, :], 0), axis=2
    )
    wanted = jnp.arange(PER_ROW, dtype=jnp.int32) * CLASSES + (rep - row) % CLASSES
    row_own = lax.dynamic_index_in_dim(own, row, 0, keepdims=False) > 0.5
    row_rank = lax.dynamic_index_in_dim(rank, row, 0, keepdims=False)
    hit = row_own[None, :] & (row_rank[None, :] == wanted[:, None])
    send = jnp.sum(jnp.where(hit, index[None, :] + 1, 0), axis=1) - 1
    my_base = lax.dynamic_index_in_dim(base, rep, 0, keepdims=False)
    my_count = lax.dynamic_index_in_dim(count, rep, 0, keepdims=False)
    place = jnp.arange(CLASS_CAP, dtype=jnp.int32)[:, None]
    inside = (place >= my_base[None, :]) & (place < (my_base + my_count)[None, :])
    arrived = index ^ (row % 2)
    keep = (
        jnp.sum(
            jnp.where(inside, arrived[None, :] * PER_ROW + place - my_base[None, :] + 1, 0), axis=1
        )
        - 1
    )
    which = (rank + index[:, None]) % CLASSES
    start = jnp.zeros_like(rank)
    for c in range(CLASSES):
        start = jnp.where(which == c, base[c][:, None] + c * CLASS_CAP, start)
    slot = start + rank // CLASSES
    slots = jnp.where(own > 0.5, slot, jnp.where(kept, slot.T + HALF, ZERO))
    a = stored
    er = lax.dynamic_index_in_dim(stored, row, 0, keepdims=False)
    k_set = er * ((index // (nb // 8)) == col)
    through = exact_dot(a * k_set[None, :], a)
    need_x = kept & ((k_set[None, :] > 0.5) | ((er[:, None] > 0.5) & (through > 0.5)))
    need_f = exact_dot(a, need_x) > 0.5
    need_f = kept & (need_f | need_f.T)
    x_slots = jnp.where(need_x, slots, ZERO)
    f_slots = jnp.where(need_f, slots, ZERO)
    pad = lambda t: jnp.pad(t, ((1, 0), (1, 0)), constant_values=ZERO)
    powers = jnp.left_shift(jnp.int32(1), index)
    bits = lambda t: jnp.pad(jnp.sum(jnp.where(t, powers[:, None], 0), axis=0), (1, 0))
    chunks = (exact_dot(a, a).astype(jnp.int32) + GROUP - 1) // GROUP
    return dict(
        send=send,
        keep=keep,
        slots=pad(slots),
        x_slots=pad(x_slots),
        f_slots=pad(f_slots),
        count=jnp.pad(chunks, ((1, 0), (1, 0))),
        near=bits(kept),
        f_bits=bits(need_f & (own > 0.5)),
        x_bits=bits(need_x),
        total=total,
    )


def pick_kernel(send_ref, got_ref, out_ref):
    for t in range(PER_ROW):
        b = send_ref[t]
        at = jnp.maximum(b, 0)
        tile = got_ref[at // 4, :, pl.ds(pl.multiple_of((at % 4) * TILE, TILE), TILE)]
        out_ref[t] = jnp.where(b >= 0, tile, jnp.zeros_like(tile))


def pack_kernel(keep_ref, all_ref, out_ref):
    def one(p, carry):
        e = keep_ref[p]
        tile = all_ref[jnp.maximum(e, 0)]
        out_ref[p] = jnp.where(e >= 0, tile, jnp.zeros_like(tile))
        return carry

    lax.fori_loop(0, CLASS_CAP, one, 0, unroll=4)


def purify_kernel(
    place_ref,
    total_ref,
    slots_ref,
    x_slots_ref,
    f_slots_ref,
    count_ref,
    near_ref,
    f_bits_ref,
    x_bits_ref,
    own_ref,
    other_ref,
    out_ref,
    w,
    f,
    x,
    todo,
    length,
    sems,
):
    row, col, core = place_ref[0], place_ref[1], place_ref[2]
    nb = 32

    def copies():
        for part, (ref, half) in enumerate(((own_ref, core), (other_ref, 1 - core))):
            for q in range(CLASSES):
                for y in range(4):
                    yield pltpu.make_async_copy(
                        ref.at[q * 4 + y],
                        w.at[pl.ds(q * CLASS_CAP, CLASS_CAP), 2 * y + half],
                        sems.at[part * 16 + q * 4 + y],
                    )

    for c in copies():
        c.start()
    zero = jnp.zeros((TILE, TILE), jnp.bfloat16)
    w[ZERO] = zero.reshape(8, CHUNK, TILE)
    f[ZERO] = zero
    x[ZERO] = zero
    def lowest(bits):
        return 32 - lax.clz(bits & -bits), bits & (bits - 1)

    for part, bits_ref in enumerate((f_bits_ref, x_bits_ref)):
        length[part, 0] = 0
        length[part, 1] = 0

        def column(j, carry, part=part, bits_ref=bits_ref):
            def add(bits):
                i, bits = lowest(bits)
                heavy = (count_ref[i, j] > 1).astype(jnp.int32)
                at = length[part, heavy]
                todo[part, heavy, at] = i * 64 + j
                length[part, heavy] = at + 1
                return bits

            lax.while_loop(lambda bits: bits != 0, add, bits_ref[j])
            return carry

        lax.fori_loop(1, nb + 1, column, 0)
        for heavy in (0, 1):
            for u in range(PAIRS):
                todo[part, heavy, length[part, heavy] + u] = 0

    for c in copies():
        c.wait()

    w_at = lambda s: w[s].reshape(TILE, TILE)
    f_at = lambda s: f[s]
    x_at = lambda s: x[s]

    for q in range(CLASSES):

        def turn(p, carry, q=q):
            for u in range(TURN):
                s = q * CLASS_CAP + p * TURN + u
                w[s + HALF] = w_at(s).T.reshape(8, CHUNK, TILE)
            return carry

        lax.fori_loop(0, (total_ref[q] + TURN - 1) // TURN, turn, 0)

    def product(pairs, chunks, left, left_slots, right, right_slots):
        def some(state):
            sums, masks = [], []
            for (i, j), bits in zip(pairs, state):
                lhs, rhs = [], []
                for _ in range(GROUP):
                    l, bits = lowest(bits)
                    lhs.append(left(left_slots[i, l]))
                    rhs.append(right(right_slots[l, j]))
                sums.append(
                    jnp.dot(
                        jnp.concatenate(lhs, axis=1),
                        jnp.concatenate(rhs, axis=0),
                        preferred_element_type=jnp.float32,
                    )
                )
                masks.append(bits)
            return sums, masks

        masks = [near_ref[i] & near_ref[j] for i, j in pairs]
        sums, masks = some(masks)
        if chunks is None:
            return sums

        def more(_, state):
            sums, masks = state
            extra, masks = some(masks)
            return [u + v for u, v in zip(sums, extra)], masks

        sums, _ = lax.fori_loop(1, chunks, more, (sums, masks))
        return sums

    def listed(part, work):
        for heavy in (0, 1):

            def some(g, carry, heavy=heavy):
                pairs = []
                for u in range(PAIRS):
                    code = todo[part, heavy, g * PAIRS + u]
                    pairs.append((code >> 6, code & 63))
                chunks = None
                if heavy:
                    chunks = most(pairs)
                work(pairs, chunks)
                return carry

            lax.fori_loop(0, (length[part, heavy] + PAIRS - 1) // PAIRS, some, 0)

    def most(pairs):
        chunks = count_ref[pairs[0][0], pairs[0][1]]
        for i, j in pairs[1:]:
            chunks = jnp.maximum(chunks, count_ref[i, j])
        return chunks

    def f_work(pairs, chunks):
        for (i, j), total in zip(pairs, product(pairs, chunks, w_at, slots_ref, w_at, slots_ref)):
            block = total.astype(jnp.bfloat16)
            f[slots_ref[i, j]] = block
            f[slots_ref[j, i]] = block.T

    def x_work(pairs, chunks):
        for (i, j), cube in zip(pairs, product(pairs, chunks, w_at, slots_ref, f_at, f_slots_ref)):
            s = x_slots_ref[i, j]
            x[s] = (1.5 * w_at(s).astype(jnp.float32) - 0.5 * cube).astype(jnp.bfloat16)

    listed(0, f_work)
    listed(1, x_work)

    for b in range(4):
        k = col * 4 + b + 1
        mine = x_slots_ref[row + 1, k]

        def some(state, k=k):
            total, bits = state
            pairs = []
            for _ in range(PAIRS):
                m, bits = lowest(bits)
                pairs.append((m, k))
            squares = product(pairs, most(pairs), x_at, x_slots_ref, x_at, x_slots_ref)
            lhs = jnp.concatenate([x[x_slots_ref[row + 1, m]] for m, _ in pairs], axis=1)
            rhs = jnp.concatenate([v.astype(jnp.bfloat16) for v in squares], axis=0)
            return total + jnp.dot(lhs, rhs, preferred_element_type=jnp.float32), bits

        bits = jnp.where(slots_ref[row + 1, k] != ZERO, near_ref[row + 1] & near_ref[k], 0)
        cube, _ = lax.while_loop(
            lambda state: state[1] != 0, some, (jnp.zeros((TILE, TILE), jnp.float32), bits)
        )
        mine = jnp.where(slots_ref[row + 1, k] != ZERO, mine, ZERO)
        out_ref[:, b * TILE : (b + 1) * TILE] = (
            1.5 * x[mine].astype(jnp.float32) - 0.5 * cube
        ).astype(jnp.bfloat16)


SMEM = pl.BlockSpec(memory_space=pltpu.SMEM)
VMEM = pl.BlockSpec(memory_space=pltpu.VMEM)
ANY = pl.BlockSpec(memory_space=pl.ANY)


def run_purify(own, other, place, table):
    bf16 = jnp.bfloat16
    return pl.pallas_call(
        purify_kernel,
        out_shape=jax.ShapeDtypeStruct((TILE, 4 * TILE), bf16),
        in_specs=[SMEM] * 9 + [ANY, ANY],
        out_specs=VMEM,
        scratch_shapes=[
            pltpu.VMEM((ZERO + 1, 8, CHUNK, TILE), bf16),
            pltpu.VMEM((ZERO + 1, TILE, TILE), bf16),
            pltpu.VMEM((ZERO + 1, TILE, TILE), bf16),
            pltpu.SMEM((2, 2, 1152), jnp.int32),
            pltpu.SMEM((2, 2), jnp.int32),
            pltpu.SemaphoreType.DMA((32,)),
        ],
        compiler_params=pltpu.CompilerParams(vmem_limit_bytes=44 * 1024 * 1024),
    )(
        place,
        table["total"],
        table["slots"],
        table["x_slots"],
        table["f_slots"],
        table["count"],
        table["near"],
        table["f_bits"],
        table["x_bits"],
        own,
        other,
    )


def sparse(density, table, row, col, rep):
    bf16 = jnp.bfloat16
    rows = lax.axis_size("row")
    got = lax.all_to_all(density.reshape(8, CHUNK, 4 * TILE), "col", 0, 0)
    picked = pl.pallas_call(
        pick_kernel,
        out_shape=jax.ShapeDtypeStruct((PER_ROW, CHUNK, TILE), bf16),
        in_specs=[SMEM, VMEM],
        out_specs=VMEM,
    )(table["send"], got)
    swapped = lax.ppermute(picked, "row", [(i, i ^ 1) for i in range(rows)])
    everywhere = lax.all_gather(
        jnp.stack([picked, swapped]),
        "row",
        axis_index_groups=[list(range(i, rows, 2)) for i in range(2)],
    ).reshape(rows * PER_ROW, CHUNK, TILE)
    packed = pl.pallas_call(
        pack_kernel,
        out_shape=jax.ShapeDtypeStruct((CLASS_CAP, CHUNK, TILE), bf16),
        in_specs=[SMEM, VMEM],
        out_specs=VMEM,
    )(table["keep"], everywhere)
    groups = [[q * 8 + c for q in range(4) for c in range(k, 8, 2)] for k in (0, 1)]
    own = lax.all_to_all(
        jnp.broadcast_to(packed[None], (16,) + packed.shape),
        ("rep", "col"),
        0,
        0,
        axis_index_groups=groups,
    )
    other = lax.ppermute(own, "col", [(i, i ^ 1) for i in range(8)])
    place = jnp.stack([row, col, col % 2]).astype(jnp.int32)
    return run_purify(own, other, place, table)


def body(density, block_mask, tile_order):
    row, col, rep = (lax.axis_index(a) for a in ("row", "col", "rep"))
    blocks = block_mask.shape[0]
    onehot = (tile_order[:, None] == jnp.arange(blocks, dtype=jnp.int32)[None, :]).astype(
        jnp.float32
    )
    stored = exact_dot(exact_dot(onehot, block_mask), onehot.T)
    own, count, fits = owners(stored, tile_order)
    return lax.cond(
        fits,
        lambda: sparse(density, tables(stored, own, count, row, col, rep), row, col, rep),
        lambda: dense(density, stored),
    )


def solution(mesh):
    return jax.shard_map(
        body,
        mesh=mesh,
        in_specs=(P("row", "col"), P(), P()),
        out_specs=P("row", "col"),
        check_vma=False,
    )
```

time: 209 us -> 151 us (0.72)
  the two profiles are of different devices: /device:TPU:2 before, /device:TPU:25 now
where the time goes in v2:
time: 151 us; the launch traced here: 150 us
  blocking collectives  63.5 us (42%)
  starting transfers between devices  29.7 us (20%)
  Pallas kernels  24.5 us (16%)
  between operations  14.7 us (10%)
  waiting for transfers between devices  7.28 us (5%)
  other arithmetic  4.76 us (3%)
  local copies, waits for them, and re-layouts  3.74 us (2%)
  matrix products  1.72 us (1%)
    all_gather x1, blocking collectives, sparse(): lax.all_gather(jnp.stack([picked, swapped]), 'row', axis_index_groups=[li...  34.1 us
    all_to_all x1, blocking collectives, sparse(): lax.all_to_all(jnp.broadcast_to(packed[None], (16,) + packed.shape), ('re...  29.4 us
    pallas_call x1, Pallas kernels, run_purify(): pl.pallas_call(purify_kernel, out_shape=jax.ShapeDtypeStruct((TILE, 4 * T...  21.2 us
    all_to_all x1, starting transfers between devices, sparse(): got = lax.all_to_all(density.reshape(8, CHUNK, 4 * TILE), 'col', 0, 0)  16.5 us
    ppermute x1, starting transfers between devices, sparse(): other = lax.ppermute(own, 'col', [(i, i ^ 1) for i in range(8)])  11.3 us
  transfers between devices with their start and end apart: 3, of which 3 were waited for; matrix products, arithmetic and copies ran while one was open for 2% of the time, Pallas kernels for 0%

profile of v2, /device:TPU:25, one launch (start us, length us, event | category | flops | bytes accessed | tf_op | source)
XLA Modules:
  0.0 150.1 jit_solution(10430168664161105725)
XLA Ops:
  6.5 0.7 broadcast_compare_fusion.2
  7.2 1.1 fusion.47
  8.3 0.6 add_reduce_fusion.1
  9.1 0.7 add_reduce_fusion
  11.2 131.5 %conditional.1 = (bf16[128,512]{1,0:T(8,128)(2,1)S(1)}) conditional(s32[]{:T(128)} %convert_element_type.85, (f32[32,32]{0,1:T(8,128)S(1)}, bf16[128,512]{1,0:T(8,128)(2,1)}) %tuple.11, (s32[]{:T(128)}, s32[]{:T(128)}, s32[4,32]{1,0:T(4,128)S(1)}, f32[32,32]{0,1:T(8,128)S(1)}, f32[32,32]{0,1:T(8,128)S(1)}, /*index=5*/s32[]{:T(128)}, ...), branch_computations={%region_4.9_spmd, %region_9.17_spmd} | conditional | flops 537985024 | bytes 38488852 | solution.py:411
  11.2 16.5 %all-to-all-start = ((bf16[8,16,512]{2,1,0:T(8,128)(2,1)}), bf16[8,16,512]{2,1,0:T(8,128)(2,1)S(1)}, u32[]{:S(2)}, u32[]{:S(2)}) async-start(bf16[8,16,512]{2,1,0:T(8,128)(2,1)} %bitcast.82), calls=%async_computation | async-start | bytes 262144 | tf_op jit(solution)/shard_map/cond/branch_1_fun/all_to_all | solution.py:371
  28.2 0.2 select_reduce_fusion.5
  28.4 0.5 broadcast_add_fusion.send_ref
  29.1 2.1 %all-to-all-done.got_ref = bf16[8,16,512]{2,1,0:T(8,128)(2,1)S(1)} async-done(((bf16[8,16,512]{2,1,0:T(8,128)(2,1)}), bf16[8,16,512]{2,1,0:T(8,128)(2,1)S(1)}, u32[]{:S(2)}, u32[]{:S(2)}) %all-to-all-start) | async-done | bytes 131104 | tf_op jit(solution)/shard_map/cond/branch_1_fun/all_to_all | solution.py:371
  31.2 0.7 copy-done.2
  31.9 1.5 %branch_1_fun.3 = bf16[3,16,128]{2,1,0:T(8,128)(2,1)} custom-call(s32[3]{0:T(128)} %broadcast_add_fusion.send_ref, bf16[8,16,512]{2,1,0:T(8,128)(2,1)} %copy-done.2), custom_call_target="tpu_custom_call" | custom-call | tf_op jit(solution)/shard_map/cond/branch_1_fun/pallas_call | solution.py:372
  33.4 1.9 %collective-permute-start = (bf16[3,16,128]{2,1,0:T(8,128)(2,1)}, bf16[3,16,128]{2,1,0:T(8,128)(2,1)S(1)}, u32[]{:S(2)}, u32[]{:S(2)}) collective-permute-start(bf16[3,16,128]{2,1,0:T(8,128)(2,1)} %branch_1_fun.3), channel_id=1, source_target_pairs={{0,32},{32,0},{64,96},{96,64},{128,160},{160,128},{192,224},{224,1... | collective-permute-start | bytes 36872 | tf_op jit(solution)/shard_map/cond/branch_1_fun/ppermute | solution.py:378
  35.3 0.5 broadcast_add_fusion.1.keep_ref
  35.8 2.2 %collective-permute-done = bf16[3,16,128]{2,1,0:T(8,128)(2,1)S(1)} collective-permute-done((bf16[3,16,128]{2,1,0:T(8,128)(2,1)}, bf16[3,16,128]{2,1,0:T(8,128)(2,1)S(1)}, u32[]{:S(2)}, u32[]{:S(2)}) %collective-permute-start) | collective-permute-done | bytes 12320 | tf_op jit(solution)/shard_map/cond/branch_1_fun/ppermute | solution.py:378
  38.0 0.7 pad_maximum_fusion
  38.8 34.1 %all-gather = bf16[32,3,16,128]{3,2,1,0:T(8,128)(2,1)} all-gather(bf16[2,3,16,128]{3,2,1,0:T(8,128)(2,1)S(1)} %pad_maximum_fusion), channel_id=2, replica_groups={{0,64,128,192,256,320,384,448,512,576,640,704,768,832,896,960},{32,96,1..., dimensions={0}, use_global_device_ids=true | all-gather | bytes 417792 | tf_op jit(solution)/shard_map/cond/branch_1_fun/all_gather | solution.py:379
  72.8 1.8 %branch_1_fun.4 = bf16[40,16,128]{2,1,0:T(8,128)(2,1)} custom-call(s32[40]{0:T(128)} %broadcast_add_fusion.1.keep_ref, bf16[96,16,128]{2,1,0:T(8,128)(2,1)} %bitcast.81), custom_call_target="tpu_custom_call" | custom-call | tf_op jit(solution)/shard_map/cond/branch_1_fun/pallas_call | solution.py:384
  74.6 1.4 broadcast_in_dim.146
  76.1 29.4 %all_to_all.8.own_ref = bf16[16,40,16,128]{3,2,1,0:T(8,128)(2,1)S(1)} all-to-all(bf16[16,40,16,128]{3,2,1,0:T(8,128)(2,1)S(1)} %broadcast_in_dim.146), channel_id=1, replica_groups={{0,8,16,24,1,9,17,25,2,10,18,26,3,11,19,27},{4,12,20,28,5,13,21,29,6,14..., dimensions={0} | all-to-all | bytes 5242880 | tf_op jit(solution)/shard_map/cond/branch_1_fun/all_to_all | solution.py:391
  105.5 11.3 %collective-permute-start.1 = (bf16[16,40,16,128]{3,2,1,0:T(8,128)(2,1)S(1)}, bf16[16,40,16,128]{3,2,1,0:T(8,128)(2,1)}, u32[]{:S(2)}, u32[]{:S(2)}) collective-permute-start(bf16[16,40,16,128]{3,2,1,0:T(8,128)(2,1)S(1)} %all_to_all.8.own_ref), channel_id=1, source_target_pairs={{0,4},{4,0},{8,12},{12,8},{16,20},{20,16},{24,28},{28,24},{1,5},{5... | collective-permute-start | bytes 7864328 | tf_op jit(solution)/shard_map/cond/branch_1_fun/ppermute | solution.py:398
  117.2 0.2 convolution_compare_fusion
  118.5 3.0 %collective-permute-done.1.other_ref = bf16[16,40,16,128]{3,2,1,0:T(8,128)(2,1)} collective-permute-done((bf16[16,40,16,128]{3,2,1,0:T(8,128)(2,1)S(1)}, bf16[16,40,16,128]{3,2,1,0:T(8,128)(2,1)}, u32[]{:S(2)}, u32[]{:S(2)}) %collective-permute-start.1) | collective-permute-done | bytes 2621472 | tf_op jit(solution)/shard_map/cond/branch_1_fun/ppermute | solution.py:398
  121.4 21.2 %branch_1_fun.5 = bf16[128,512]{1,0:T(8,128)(2,1)S(1)} custom-call(s32[3]{0:T(128)S(1)} %pad_add_fusion.place_ref, s32[4]{0:T(128)S(1)} %reduce_sum.72.total_ref, s32[33,33]{1,0:T(8,128)S(1)} %pad.16.slots_ref, s32[33,33]{1,0:T(8,128)S(1)} %pad.17.x_slots_ref, s32[33,33]{1,0:T(8,128)S(1)} %pad.18.f_slots_ref, s32[33,33]{1,0:T(8,128)S(1)} %pad.19.count_ref, ...), custom_call_target="tpu_custom_call" | custom-call | tf_op jit(solution)/shard_map/cond/branch_1_fun/pallas_call | solution.py:339
  142.6 0.6 copy-done.3
  (34 shorter events, 2.2 us)
Async XLA Ops:
  11.2 20.0 %all-to-all-start = ((bf16[8,16,512]{2,1,0:T(8,128)(2,1)}), bf16[8,16,512]{2,1,0:T(8,128)(2,1)S(1)}, u32[]{:S(2)}, u32[]{:S(2)}) async-start(bf16[8,16,512]{2,1,0:T(8,128)(2,1)} %bitcast.82), calls=%async_computation | async-start | bytes 262144 | tf_op jit(solution)/shard_map/cond/branch_1_fun/all_to_all | solution.py:371
  31.2 0.7 copy-start.2
  33.4 4.6 %collective-permute-start = (bf16[3,16,128]{2,1,0:T(8,128)(2,1)}, bf16[3,16,128]{2,1,0:T(8,128)(2,1)S(1)}, u32[]{:S(2)}, u32[]{:S(2)}) collective-permute-start(bf16[3,16,128]{2,1,0:T(8,128)(2,1)} %branch_1_fun.3), channel_id=1, source_target_pairs={{0,32},{32,0},{64,96},{96,64},{128,160},{160,128},{192,224},{224,1... | collective-permute-start | bytes 36872 | tf_op jit(solution)/shard_map/cond/branch_1_fun/ppermute | solution.py:378
  105.5 16.0 %collective-permute-start.1 = (bf16[16,40,16,128]{3,2,1,0:T(8,128)(2,1)S(1)}, bf16[16,40,16,128]{3,2,1,0:T(8,128)(2,1)}, u32[]{:S(2)}, u32[]{:S(2)}) collective-permute-start(bf16[16,40,16,128]{3,2,1,0:T(8,128)(2,1)S(1)} %all_to_all.8.own_ref), channel_id=1, source_target_pairs={{0,4},{4,0},{8,12},{12,8},{16,20},{20,16},{24,28},{28,24},{1,5},{5... | collective-permute-start | bytes 7864328 | tf_op jit(solution)/shard_map/cond/branch_1_fun/ppermute | solution.py:398
  142.6 0.7 copy-start.3
